TPU v7x, 32 devices: a whole 2x2x4 slice. The times are simulated.
32 devices in a mesh: replica: 16 (over z, y, core), tensor: 2 (over x).
Axes of the slice: x: 2, y: 2, z: 4, core: 2. Of those that a mesh axis runs over, the one named last changes fastest.
Arguments:
- prefill_q: bfloat16 [6144, 8192], P('replica', 'tensor'), may hold values from -16 to 16
- decode_q: bfloat16 [32, 8192], P('replica', 'tensor'), may hold values from -16 to 16
- overflow_q: bfloat16 [96, 8192], P('replica', 'tensor'), may hold values from -16 to 16
- key_pool: bfloat16 [67584, 1024], P('replica', 'tensor'), may hold values from -10 to 10
- value_pool: bfloat16 [67584, 1024], P('replica', 'tensor'), may hold values from -6 to 6
- prefill_pages: int32 [16, 19], P('replica'), may hold values from 0 to 32, as said below
- decode_pages: int32 [32, 4], P('replica'), may hold values from 0 to 32, as said below
- decode_len: int32 [32], P('replica'), may hold values from 1 to 512, as said below
- overflow_pages: int32 [96], P('replica'), may hold values from 0 to 32, as said below
- overflow_len: int32 [96], P('replica'), may hold values from 1 to 128, as said below
- overflow_dest: int32 [96], P('replica'), may hold values from 0 to 15, as said below
Outputs:
- prefill_out: bfloat16 [6144, 8192], P(('replica', 'tensor'))
- decode_out: bfloat16 [32, 8192], P('replica', 'tensor')
- moved_out: bfloat16 [256, 8192], P('replica', 'tensor')
Inputs may be any that keep to these rules, and one draw needn't show every extreme that they name: The page lists of one replica (prefill_pages, decode_pages and overflow_pages together) name distinct pages of that replica's pool. `decode_pages`: distinct pages of the own pool, as for prefill_pages. `overflow_pages`: distinct pages of the own pool, as for prefill_pages. `decode_len`: every replica has a decoding request of exactly 512 positions. `overflow_len`: every replica has an overflow request of exactly 128 positions. `overflow_dest`: the requests of one replica go to distinct replicas other than itself; one replica receives a request from every other replica.
All inputs are finite; a program needn't handle non-finite values.
Results may differ from a plain program's by a relative error of at most 0.0049.
Values may be sent and summed in bfloat16 or wider, within the bound.
No kernel may reach another device: no remote copies, remote signals or barrier semaphores. Data moves between devices by JAX's collectives and lax.ppermute only.
A program may use at most 128 MiB of HBM per device.

v0:
```python
import functools
import math

import jax
import jax.numpy as jnp
from jax import lax
from jax.experimental import pallas as pl
from jax.experimental.pallas import tpu as pltpu
from jax.sharding import PartitionSpec as P

Q_HEADS = 64
KV_HEADS = 8
D_HEAD = 128
PAGE = 128
GROUP = Q_HEADS // KV_HEADS
SCALE = math.log2(math.e) / math.sqrt(D_HEAD)
LOW = -1e30
CHUNK = 512
VMEM_LIMIT = 60 * 2**20

NT = (((1,), (1,)), ((), ()))


def chunks_of(earlier, tail):
    starts = list(range(0, earlier, CHUNK)) + [earlier]
    return [(a, b - a) for a, b in zip(starts, starts[1:] + [earlier + tail])]


def prefill_kernel(
    tail, blk_ref, pages_ref, q_ref, k_hbm, v_hbm, o_ref,
    kbuf, vbuf, score, top, acc, sem, *, first, pack
):
    heads = kbuf.shape[0]
    count = pages_ref.shape[0]
    span = count * PAGE
    rows = q_ref.shape[0]
    units = GROUP // pack
    pieces = chunks_of(span - tail, tail)

    def fetch(head):
        cols = pl.ds(pl.multiple_of((first + head) * D_HEAD, D_HEAD), D_HEAD)

        def one(j, _):
            src = pl.ds(pl.multiple_of(pages_ref[j] * PAGE, PAGE), PAGE)
            dst = pl.ds(pl.multiple_of(j * PAGE, PAGE), PAGE)
            pltpu.make_async_copy(k_hbm.at[src, cols], kbuf.at[head, dst], sem.at[head, 0]).start()
            pltpu.make_async_copy(v_hbm.at[src, cols], vbuf.at[head, dst], sem.at[head, 1]).start()
            return 0

        lax.fori_loop(0, count, one, 0)

    def keys_ready(head):
        pltpu.make_async_copy(kbuf.at[head], kbuf.at[head], sem.at[head, 0]).wait()

    def values_ready(head):
        pltpu.make_async_copy(vbuf.at[head], vbuf.at[head], sem.at[head, 1]).wait()

    def columns(unit, h):
        return pl.ds(pl.multiple_of((unit * pack + h) * D_HEAD, D_HEAD), D_HEAD)

    def across(x, size):
        return jnp.concatenate([x] * (size // D_HEAD), axis=1)

    def fold(op, kept, x):
        for at in range(0, x.shape[1], D_HEAD):
            piece = x[:, at:at + D_HEAD]
            kept = piece if kept is None else op(kept, piece)
        return kept

    def tops(u):
        return pl.when(u >= 0)

    def unit(u, _):
        head = u // units

        @pl.when((u % units == 0) & (head + 1 < heads))
        def _():
            fetch(head + 1)

        @pl.when(u % units == 0)
        def _():
            keys_ready(head)

        for i, (start, size) in enumerate(pieces):

            @tops(u)
            def _(i=i, start=start, size=size):
                q = jnp.concatenate([q_ref[:, columns(u, h)] for h in range(pack)], axis=0)
                keys = kbuf[head, start:start + size, :]
                s = lax.dot_general(q, keys, NT, preferred_element_type=jnp.float32)
                if start >= span - tail:
                    usable = lax.broadcasted_iota(jnp.int32, (rows, size), 1) <= (
                        lax.broadcasted_iota(jnp.int32, (rows, size), 0)
                        + (blk_ref[0] * rows + span - tail - start)
                    )
                    s = jnp.where(usable[None], s.reshape(pack, rows, size), LOW).reshape(s.shape)
                score[:, start:start + size] = s
                peak = fold(jnp.maximum, None, s)
                if i > 0:
                    peak = jnp.maximum(peak, top[...])
                if start + size == span:
                    peak = jnp.max(peak, axis=1, keepdims=True) * SCALE
                    peak = jnp.broadcast_to(peak, top.shape)
                top[...] = peak

        @pl.when(u % units == 0)
        def _():
            values_ready(head)

        for i, (start, size) in enumerate(pieces):

            @tops(u)
            def _(i=i, start=start, size=size):
                x = score[:, start:start + size]
                p = jnp.exp2(x * SCALE - across(top[...], size))
                values = vbuf[head, start:start + size, :]
                values = jnp.concatenate([values, jnp.ones_like(values)], axis=1)
                o = jnp.dot(p.astype(jnp.bfloat16), values, preferred_element_type=jnp.float32)
                if i > 0:
                    o = o + acc[...]
                if start + size < span:
                    acc[...] = o
                else:
                    o = (o[:, :D_HEAD] / o[:, D_HEAD:]).astype(o_ref.dtype)
                    for h in range(pack):
                        o_ref[:, columns(u, h)] = o[h * rows:(h + 1) * rows]

        return 0

    fetch(0)
    lax.fori_loop(0, heads * units, unit, 0)


def prefill_part(q, keys, values, pages, blk, ranks, first, heads, pack, wide=False):
    tokens = q.shape[0]
    rows = tokens // ranks
    span = pages.shape[0] * PAGE
    width = heads * GROUP * D_HEAD
    total = ranks * keys.shape[1] // D_HEAD // heads if wide else 1
    work = heads * GROUP * rows * span

    return pl.pallas_call(
        functools.partial(prefill_kernel, tokens, first=first, pack=pack),
        grid_spec=pltpu.PrefetchScalarGridSpec(
            num_scalar_prefetch=2,
            grid=(1,),
            in_specs=[
                pl.BlockSpec((rows, width), lambda i, blk, pages: (blk[0], first // heads)),
                pl.BlockSpec(memory_space=pl.ANY),
                pl.BlockSpec(memory_space=pl.ANY),
            ],
            out_specs=pl.BlockSpec((rows, width), lambda i, blk, pages: (0, blk[0] if wide else 0)),
            scratch_shapes=[
                pltpu.VMEM((heads, span, D_HEAD), jnp.bfloat16),
                pltpu.VMEM((heads, span, D_HEAD), jnp.bfloat16),
                pltpu.VMEM((pack * rows, span), jnp.float32),
                pltpu.VMEM((pack * rows, D_HEAD), jnp.float32),
                pltpu.VMEM((pack * rows, 2 * D_HEAD), jnp.float32),
                pltpu.SemaphoreType.DMA((heads, 2)),
            ],
        ),
        out_shape=jax.ShapeDtypeStruct((rows, total * width), q.dtype),
        compiler_params=pltpu.CompilerParams(vmem_limit_bytes=VMEM_LIMIT),
        cost_estimate=pl.CostEstimate(
            flops=4 * work * D_HEAD,
            bytes_accessed=4 * (heads * span * D_HEAD + rows * width),
            transcendentals=work,
        ),
        name="prefill",
    )(blk, pages, q, keys, values)


def small_kernel(
    over_pages, dec_pages, over_len, dec_len, dest_ref, over_ref, decq_ref, k_hbm, v_hbm,
    dec_ref, out_ref, kbuf, vbuf, q_all, res, flat, sem
):
    over, (dec, per) = over_pages.shape[0], dec_pages.shape
    count = over + dec * per
    batch = q_all.shape[0]
    keys = count * PAGE
    heads = q_all.shape[1] // D_HEAD

    for j in range(count):
        page = over_pages[j] if j < over else dec_pages[(j - over) // per, (j - over) % per]
        src = pl.ds(pl.multiple_of(page * PAGE, PAGE), PAGE)
        dst = pl.ds(j * PAGE, PAGE)
        pltpu.make_async_copy(k_hbm.at[src], kbuf.at[dst], sem.at[0]).start()
        pltpu.make_async_copy(v_hbm.at[src], vbuf.at[dst], sem.at[1]).start()

    if batch > over + dec:
        q_all[...] = jnp.zeros_like(q_all)
    q_all[0:over, :] = over_ref[...].astype(jnp.float32)
    q_all[over:over + dec, :] = decq_ref[...].astype(jnp.float32)
    out_ref[...] = jnp.zeros_like(out_ref)
    row = lax.broadcasted_iota(jnp.int32, (batch, PAGE), 0)
    lane = lax.broadcasted_iota(jnp.int32, (batch, PAGE), 1)
    masks = []
    for j in range(count):
        owner, base = (j, 0) if j < over else (over + (j - over) // per, (j - over) % per * PAGE)
        most = over_len[j] if j < over else dec_len[owner - over]
        masks.append((row == owner) & (lane + base < most))
    pltpu.make_async_copy(kbuf, kbuf, sem.at[0]).wait()
    for g in range(k_hbm.shape[1] // D_HEAD):
        cols = slice(g * D_HEAD, (g + 1) * D_HEAD)
        q = jnp.concatenate(
            [q_all[:, (g * GROUP + h) * D_HEAD:(g * GROUP + h + 1) * D_HEAD] for h in range(GROUP)],
            axis=0,
        ).astype(jnp.bfloat16)
        s = lax.dot_general(q, kbuf[:, cols], NT, preferred_element_type=jnp.float32)
        s = s.reshape(GROUP, batch, keys)
        s = jnp.concatenate(
            [
                jnp.where(masks[j][None], s[:, :, j * PAGE:(j + 1) * PAGE], LOW)
                for j in range(count)
            ],
            axis=2,
        ).reshape(GROUP * batch, keys)
        p = jnp.exp2((s - jnp.max(s, axis=1, keepdims=True)) * SCALE)
        total = jnp.sum(p, axis=1, keepdims=True)
        w = (p / total).astype(jnp.bfloat16)
        if g == 0:
            pltpu.make_async_copy(vbuf, vbuf, sem.at[1]).wait()
        o = jnp.dot(w, vbuf[:, cols], preferred_element_type=jnp.float32)
        for h in range(GROUP):
            at = g * GROUP + h
            res[:, at * D_HEAD:(at + 1) * D_HEAD] = o[h * batch:(h + 1) * batch]
            flat[pl.ds(at, batch, stride=heads), :] = o[h * batch:(h + 1) * batch]
    dec_ref[...] = res[over:over + dec, :].astype(dec_ref.dtype)
    for m in range(over):
        out_ref[dest_ref[m]] = flat[m * heads:(m + 1) * heads, :].astype(out_ref.dtype)


def small_part(decode_q, overflow_q, keys, values, dec_pages, over_pages, dec_len, over_len, dest, replicas):
    dec, over = decode_q.shape[0], overflow_q.shape[0]
    batch = -(-(dec + over) // 8) * 8
    width = decode_q.shape[1]
    span = (over + dec_pages.size) * PAGE
    work = batch * width * span
    moved = (replicas, width // D_HEAD, D_HEAD)
    return pl.pallas_call(
        small_kernel,
        grid_spec=pltpu.PrefetchScalarGridSpec(
            num_scalar_prefetch=5,
            grid=(1,),
            in_specs=[
                pl.BlockSpec((over, width), lambda i, *_: (0, 0)),
                pl.BlockSpec((dec, width), lambda i, *_: (0, 0)),
                pl.BlockSpec(memory_space=pl.ANY),
                pl.BlockSpec(memory_space=pl.ANY),
            ],
            out_specs=[
                pl.BlockSpec((dec, width), lambda i, *_: (0, 0)),
                pl.BlockSpec(moved, lambda i, *_: (0, 0, 0)),
            ],
            scratch_shapes=[
                pltpu.VMEM((span, keys.shape[1]), jnp.bfloat16),
                pltpu.VMEM((span, keys.shape[1]), jnp.bfloat16),
                pltpu.VMEM((batch, width), jnp.float32),
                pltpu.VMEM((batch, width), jnp.float32),
                pltpu.VMEM((batch * width // D_HEAD, D_HEAD), jnp.float32),
                pltpu.SemaphoreType.DMA((2,)),
            ],
        ),
        out_shape=[
            jax.ShapeDtypeStruct((dec, width), decode_q.dtype),
            jax.ShapeDtypeStruct(moved, decode_q.dtype),
        ],
        compiler_params=pltpu.CompilerParams(vmem_limit_bytes=VMEM_LIMIT),
        cost_estimate=pl.CostEstimate(
            flops=4 * work, bytes_accessed=4 * span * keys.shape[1], transcendentals=work // D_HEAD
        ),
        name="small",
    )(over_pages, dec_pages, over_len, dec_len, dest, overflow_q, decode_q, keys, values)


def finish_kernel(ranks, rank_ref, rows_ref, big_ref, *refs):
    got, (out_ref, mov_ref, flat, sem) = refs[:-4], refs[-4:]
    del big_ref
    cols = got[0].shape[1]
    heads = len(got) // (ranks - 1)
    copies = []
    for i, part in enumerate(got):
        source = lax.rem(rank_ref[0] + ranks - (i // heads + 1), ranks)
        to = pl.ds(pl.multiple_of((source * heads + i % heads) * cols, cols), cols)
        copies.append(pltpu.make_async_copy(part, out_ref.at[:, to], sem.at[i]))
        copies[-1].start()
    replicas, count, _ = rows_ref.shape
    flat[...] = rows_ref[...].astype(jnp.float32).reshape(flat.shape)
    for h in range(count):
        line = flat[pl.ds(h, replicas, stride=count), :]
        mov_ref[:, h * D_HEAD:(h + 1) * D_HEAD] = line.astype(mov_ref.dtype)
    for copy in copies:
        copy.wait()


def finish_part(rank, ranks, rows, big, got):
    replicas, count, _ = rows.shape
    anywhere = pl.BlockSpec(memory_space=pl.ANY)
    return pl.pallas_call(
        functools.partial(finish_kernel, ranks),
        grid_spec=pltpu.PrefetchScalarGridSpec(
            num_scalar_prefetch=1,
            grid=(1,),
            in_specs=[pl.BlockSpec(rows.shape, lambda i, *_: (0, 0, 0)), anywhere]
            + [pl.BlockSpec(memory_space=pltpu.VMEM)] * len(got),
            out_specs=[anywhere, pl.BlockSpec((replicas, count * D_HEAD), lambda i, *_: (0, 0))],
            scratch_shapes=[
                pltpu.VMEM((replicas * count, D_HEAD), jnp.float32),
                pltpu.SemaphoreType.DMA((len(got),)),
            ],
        ),
        out_shape=[
            jax.ShapeDtypeStruct(big.shape, big.dtype),
            jax.ShapeDtypeStruct((replicas, count * D_HEAD), big.dtype),
        ],
        input_output_aliases={2: 0},
        compiler_params=pltpu.CompilerParams(vmem_limit_bytes=16 * 2**20),
        cost_estimate=pl.CostEstimate(
            flops=0, bytes_accessed=2 * big.size + 4 * rows.size, transcendentals=0
        ),
        name="finish",
    )(rank, rows, big, *got)


def per_device(
    prefill_q,
    decode_q,
    overflow_q,
    key_pool,
    value_pool,
    prefill_pages,
    decode_pages,
    decode_len,
    overflow_pages,
    overflow_len,
    overflow_dest,
):
    ranks, replicas = lax.axis_size("tensor"), lax.axis_size("replica")
    rank = lax.axis_index("tensor")
    heads = key_pool.shape[1] // D_HEAD
    pages = prefill_pages[0]

    decode_out, sent = small_part(
        decode_q,
        overflow_q,
        key_pool,
        value_pool,
        decode_pages,
        overflow_pages,
        decode_len,
        overflow_len,
        overflow_dest,
        replicas,
    )
    sent, pages = lax.optimization_barrier((sent, pages))
    rows = lax.all_to_all(sent, "replica", split_axis=0, concat_axis=0, tiled=True)

    got = []
    for shift in range(1, ranks):
        blk = lax.rem(rank + shift, ranks)[None].astype(jnp.int32)
        step = min(heads, 2)
        for g in range(0, heads, step):
            part = prefill_part(
                prefill_q, key_pool, value_pool, pages, blk, ranks, g, step, pack=4
            )
            got.append(lax.ppermute(part, "tensor", [(i, (i + shift) % ranks) for i in range(ranks)]))
    own = rank[None].astype(jnp.int32)
    prefill_out = prefill_part(
        prefill_q, key_pool, value_pool, pages, own, ranks, 0, heads, pack=8, wide=True
    )
    prefill_out, moved_out = finish_part(own, ranks, rows, prefill_out, got)
    return (prefill_out, decode_out, moved_out)


def solution(mesh):
    in_specs = (
        P("replica", "tensor"),
        P("replica", "tensor"),
        P("replica", "tensor"),
        P("replica", "tensor"),
        P("replica", "tensor"),
        P("replica", None),
        P("replica", None),
        P("replica"),
        P("replica"),
        P("replica"),
        P("replica"),
    )
    out_specs = (P(("replica", "tensor"), None), P("replica", "tensor"), P("replica", "tensor"))
    return jax.shard_map(
        per_device, mesh=mesh, in_specs=in_specs, out_specs=out_specs, check_vma=False
    )
```

profile of v0, /device:TPU:0, one launch (start us, length us, event | category | flops | bytes accessed | tf_op | source)
XLA Modules:
  0.0 70.4 jit_solution(9198807278085301031)
XLA Ops:
  0.6 6.6 %small.1 = (bf16[2,4096]{1,0:T(2,128)(2,1)}, bf16[16,32,128]{2,1,0:T(8,128)(2,1)}) custom-call(s32[6]{0:T(128)} %over_pages.1, s32[2,4]{1,0:T(2,128)} %dec_pages.1, s32[6]{0:T(128)} %over_len.1, s32[2]{0:T(128)} %dec_len.1, s32[6]{0:T(128)} %dest_ref.1, bf16[6,4096]{1,0:T(8,128)(2,1)} %over_ref.1, bf16[2,4096]{1,0:T(2,128)(2,1)} %decq_ref.1, ...), custom_call_target="tpu_custom_call" | custom-call | flops 234881024 | bytes 3670016 | tf_op jit(solution)/shard_map/small/pallas_call | solution.py:240
  7.3 13.8 %prefill.4 = bf16[192,2048]{1,0:T(8,128)(2,1)} custom-call(s32[1]{0:T(128)} %bitcast.2.blk_ref, s32[19]{0:T(128)} %bitcast.3, bf16[384,4096]{1,0:T(8,128)(2,1)} %q_ref.5, bf16[4224,512]{1,0:T(8,128)(2,1)} %k_hbm.7, bf16[4224,512]{1,0:T(8,128)(2,1)} %v_hbm.7), custom_call_target="tpu_custom_call" | custom-call | flops 3825205248 | bytes 4063232 | tf_op jit(solution)/shard_map/prefill/pallas_call | solution.py:142
  21.1 3.0 %collective-permute-start = (bf16[192,2048]{1,0:T(8,128)(2,1)}, bf16[192,2048]{1,0:T(8,128)(2,1)S(1)}, u32[]{:S(2)}, u32[]{:S(2)}) collective-permute-start(bf16[192,2048]{1,0:T(8,128)(2,1)} %prefill.4), channel_id=1, source_target_pairs={{0,1},{1,0},{2,3},{3,2},{4,5},{5,4},{6,7},{7,6},{8,9},{9,8},{10,11... | collective-permute-start | bytes 2359304 | tf_op jit(solution)/shard_map/ppermute | solution.py:366
  24.1 13.8 %prefill.5 = bf16[192,2048]{1,0:T(8,128)(2,1)} custom-call(s32[1]{0:T(128)} %bitcast.2.blk_ref, s32[19]{0:T(128)} %bitcast.4, bf16[384,4096]{1,0:T(8,128)(2,1)} %q_ref.5, bf16[4224,512]{1,0:T(8,128)(2,1)} %k_hbm.7, bf16[4224,512]{1,0:T(8,128)(2,1)} %v_hbm.7), custom_call_target="tpu_custom_call" | custom-call | flops 3825205248 | bytes 4063232 | tf_op jit(solution)/shard_map/prefill/pallas_call | solution.py:142
  37.9 0.1 collective-permute-start.1
  38.0 6.5 %all-to-all-start = ((bf16[16,32,128]{2,1,0:T(8,128)(2,1)}), bf16[16,32,128]{2,1,0:T(8,128)(2,1)S(1)}, u32[]{:S(2)}, u32[]{:S(2)}) async-start(bf16[16,32,128]{2,1,0:T(8,128)(2,1)} %get-tuple-element.10), calls=%async_computation | async-start | bytes 262144 | tf_op jit(solution)/shard_map/all_to_all | solution.py:356
  44.4 23.9 %prefill.3.big_ref = bf16[192,8192]{1,0:T(8,128)(2,1)} custom-call(s32[1]{0:T(128)} %bitcast.blk_ref.rank_ref, s32[19]{0:T(128)} %bitcast.5, bf16[384,4096]{1,0:T(8,128)(2,1)} %q_ref.5, bf16[4224,512]{1,0:T(8,128)(2,1)} %k_hbm.7, bf16[4224,512]{1,0:T(8,128)(2,1)} %v_hbm.7), custom_call_target="tpu_custom_call" | custom-call | flops 7650410496 | bytes 8126464 | tf_op jit(solution)/shard_map/prefill/pallas_call | solution.py:142
  68.4 0.0 all-to-all-done.rows_ref
  68.4 0.0 collective-permute-done.refs_0_
  68.4 0.0 collective-permute-done.1.refs_1_
  68.4 1.8 %finish.1 = (bf16[192,8192]{1,0:T(8,128)(2,1)}, bf16[16,4096]{1,0:T(8,128)(2,1)}) custom-call(s32[1]{0:T(128)} %bitcast.blk_ref.rank_ref, bf16[16,32,128]{2,1,0:T(8,128)(2,1)S(1)} %all-to-all-done.rows_ref, bf16[192,8192]{1,0:T(8,128)(2,1)} %prefill.3.big_ref, bf16[192,2048]{1,0:T(8,128)(2,1)S(1)} %collective-permute-done.refs_0_, ...), custom_call_target="tpu_custom_call", output_to_operand_aliasing={{0}: (2, {})} | custom-call | bytes 3407872 | tf_op jit(solution)/shard_map/finish/pallas_call | solution.py:299
Async XLA Ops:
  21.1 47.3 %collective-permute-start = (bf16[192,2048]{1,0:T(8,128)(2,1)}, bf16[192,2048]{1,0:T(8,128)(2,1)S(1)}, u32[]{:S(2)}, u32[]{:S(2)}) collective-permute-start(bf16[192,2048]{1,0:T(8,128)(2,1)} %prefill.4), channel_id=1, source_target_pairs={{0,1},{1,0},{2,3},{3,2},{4,5},{5,4},{6,7},{7,6},{8,9},{9,8},{10,11... | collective-permute-start | bytes 2359304 | tf_op jit(solution)/shard_map/ppermute | solution.py:366
  37.9 30.5 %collective-permute-start.1 = (bf16[192,2048]{1,0:T(8,128)(2,1)}, bf16[192,2048]{1,0:T(8,128)(2,1)S(1)}, u32[]{:S(2)}, u32[]{:S(2)}) collective-permute-start(bf16[192,2048]{1,0:T(8,128)(2,1)} %prefill.5), channel_id=1, source_target_pairs={{0,1},{1,0},{2,3},{3,2},{4,5},{5,4},{6,7},{7,6},{8,9},{9,8},{10,11... | collective-permute-start | bytes 2359304 | tf_op jit(solution)/shard_map/ppermute | solution.py:366
  38.0 30.4 %all-to-all-start = ((bf16[16,32,128]{2,1,0:T(8,128)(2,1)}), bf16[16,32,128]{2,1,0:T(8,128)(2,1)S(1)}, u32[]{:S(2)}, u32[]{:S(2)}) async-start(bf16[16,32,128]{2,1,0:T(8,128)(2,1)} %get-tuple-element.10), calls=%async_computation | async-start | bytes 262144 | tf_op jit(solution)/shard_map/all_to_all | solution.py:356
where the time goes:
time: 71.1 us; the launch traced here: 70.4 us
  Pallas kernels  60 us (84%)
  starting transfers between devices  9.55 us (13%)
  between operations  0.86 us (1%)
    pallas_call x3, Pallas kernels, prefill_part(): pl.pallas_call(functools.partial(prefill_kernel, tokens, first=first, pac...  51.5 us
    pallas_call x1, Pallas kernels, small_part(): pl.pallas_call(small_kernel, grid_spec=pltpu.PrefetchScalarGridSpec(num_s...  6.63 us
    all_to_all x1, starting transfers between devices, per_device(): lax.all_to_all(sent, 'replica', split_axis=0, concat_axis=0, tiled=True)  6.47 us
    ppermute x2, starting transfers between devices, per_device(): lax.ppermute(part, 'tensor', [(i, (i + shift) % ranks) for i in range(ran...  3.09 us
    pallas_call x1, Pallas kernels, finish_part(): pl.pallas_call(functools.partial(finish_kernel, ranks), grid_spec=pltpu.P...  1.82 us
  transfers between devices with their start and end apart: 3, of which 0 were waited for; matrix products, arithmetic and copies ran while one was open for 0% of the time, Pallas kernels for 54%

commit v1 on v0

--- a/solution.py
+++ b/solution.py
@@ -40,14 +40,17 @@
     def fetch(head):
         cols = pl.ds(pl.multiple_of((first + head) * D_HEAD, D_HEAD), D_HEAD)
 
-        def one(j, _):
-            src = pl.ds(pl.multiple_of(pages_ref[j] * PAGE, PAGE), PAGE)
-            dst = pl.ds(pl.multiple_of(j * PAGE, PAGE), PAGE)
-            pltpu.make_async_copy(k_hbm.at[src, cols], kbuf.at[head, dst], sem.at[head, 0]).start()
-            pltpu.make_async_copy(v_hbm.at[src, cols], vbuf.at[head, dst], sem.at[head, 1]).start()
-            return 0
-
-        lax.fori_loop(0, count, one, 0)
+        for kind, (pool, buf) in enumerate(((k_hbm, kbuf), (v_hbm, vbuf))):
+
+            def one(j, _):
+                src = pl.ds(pl.multiple_of(pages_ref[j] * PAGE, PAGE), PAGE)
+                dst = pl.ds(pl.multiple_of(j * PAGE, PAGE), PAGE)
+                pltpu.make_async_copy(
+                    pool.at[src, cols], buf.at[head, dst], sem.at[head, kind]
+                ).start()
+                return 0
+
+            lax.fori_loop(0, count, one, 0)
 
     def keys_ready(head):
         pltpu.make_async_copy(kbuf.at[head], kbuf.at[head], sem.at[head, 0]).wait()
@@ -172,7 +175,7 @@
 
 def small_kernel(
     over_pages, dec_pages, over_len, dec_len, dest_ref, over_ref, decq_ref, k_hbm, v_hbm,
-    dec_ref, out_ref, kbuf, vbuf, q_all, res, flat, sem
+    dec_ref, out_ref, kbuf, vbuf, q_all, res, bias, flat, sem
 ):
     over, (dec, per) = over_pages.shape[0], dec_pages.shape
     count = over + dec * per
@@ -194,37 +197,36 @@
     out_ref[...] = jnp.zeros_like(out_ref)
     row = lax.broadcasted_iota(jnp.int32, (batch, PAGE), 0)
     lane = lax.broadcasted_iota(jnp.int32, (batch, PAGE), 1)
-    masks = []
     for j in range(count):
         owner, base = (j, 0) if j < over else (over + (j - over) // per, (j - over) % per * PAGE)
         most = over_len[j] if j < over else dec_len[owner - over]
-        masks.append((row == owner) & (lane + base < most))
+        valid = (row == owner) & (lane + base < most)
+        bias[:, j * PAGE:(j + 1) * PAGE] = jnp.where(valid, 0.0, LOW)
     pltpu.make_async_copy(kbuf, kbuf, sem.at[0]).wait()
-    for g in range(k_hbm.shape[1] // D_HEAD):
-        cols = slice(g * D_HEAD, (g + 1) * D_HEAD)
+    pltpu.make_async_copy(vbuf, vbuf, sem.at[1]).wait()
+
+    def head(g, _):
+        cols = pl.ds(pl.multiple_of(g * D_HEAD, D_HEAD), D_HEAD)
         q = jnp.concatenate(
-            [q_all[:, (g * GROUP + h) * D_HEAD:(g * GROUP + h + 1) * D_HEAD] for h in range(GROUP)],
+            [
+                q_all[:, pl.ds(pl.multiple_of((g * GROUP + h) * D_HEAD, D_HEAD), D_HEAD)]
+                for h in range(GROUP)
+            ],
             axis=0,
         ).astype(jnp.bfloat16)
         s = lax.dot_general(q, kbuf[:, cols], NT, preferred_element_type=jnp.float32)
-        s = s.reshape(GROUP, batch, keys)
-        s = jnp.concatenate(
-            [
-                jnp.where(masks[j][None], s[:, :, j * PAGE:(j + 1) * PAGE], LOW)
-                for j in range(count)
-            ],
-            axis=2,
-        ).reshape(GROUP * batch, keys)
+        s = (s.reshape(GROUP, batch, keys) + bias[...][None]).reshape(GROUP * batch, keys)
         p = jnp.exp2((s - jnp.max(s, axis=1, keepdims=True)) * SCALE)
-        total = jnp.sum(p, axis=1, keepdims=True)
-        w = (p / total).astype(jnp.bfloat16)
-        if g == 0:
-            pltpu.make_async_copy(vbuf, vbuf, sem.at[1]).wait()
+        w = (p / jnp.sum(p, axis=1, keepdims=True)).astype(jnp.bfloat16)
         o = jnp.dot(w, vbuf[:, cols], preferred_element_type=jnp.float32)
         for h in range(GROUP):
             at = g * GROUP + h
-            res[:, at * D_HEAD:(at + 1) * D_HEAD] = o[h * batch:(h + 1) * batch]
-            flat[pl.ds(at, batch, stride=heads), :] = o[h * batch:(h + 1) * batch]
+            part = o[h * batch:(h + 1) * batch]
+            res[:, pl.ds(pl.multiple_of(at * D_HEAD, D_HEAD), D_HEAD)] = part
+            flat[pl.ds(at, batch, stride=heads), :] = part
+        return 0
+
+    lax.fori_loop(0, k_hbm.shape[1] // D_HEAD, head, 0)
     dec_ref[...] = res[over:over + dec, :].astype(dec_ref.dtype)
     for m in range(over):
         out_ref[dest_ref[m]] = flat[m * heads:(m + 1) * heads, :].astype(out_ref.dtype)
@@ -257,6 +259,7 @@
                 pltpu.VMEM((span, keys.shape[1]), jnp.bfloat16),
                 pltpu.VMEM((batch, width), jnp.float32),
                 pltpu.VMEM((batch, width), jnp.float32),
+                pltpu.VMEM((batch, span), jnp.float32),
                 pltpu.VMEM((batch * width // D_HEAD, D_HEAD), jnp.float32),
                 pltpu.SemaphoreType.DMA((2,)),
             ],
@@ -361,7 +364,7 @@
         step = min(heads, 2)
         for g in range(0, heads, step):
             part = prefill_part(
-                prefill_q, key_pool, value_pool, pages, blk, ranks, g, step, pack=4
+                prefill_q, key_pool, value_pool, pages, blk, ranks, g, step, pack=8
             )
             got.append(lax.ppermute(part, "tensor", [(i, (i + shift) % ranks) for i in range(ranks)]))
     own = rank[None].astype(jnp.int32)

time: 71.1 us -> 70.5 us (level)
    pallas_call x3, Pallas kernels: 51.5 us -> 50.4 us  [prefill_part(): pl.pallas_call(functools.partial(prefill_kernel, tokens, first=first, pac...]
  transfers between devices with their start and end apart: 3 -> 3, of which waited for: 0 -> 0; matrix products, arithmetic and copies ran while one was open for 0% -> 0% of each run, Pallas kernels for 54% -> 53%
where the time goes in v1:
time: 70.5 us; the launch traced here: 69.8 us
  Pallas kernels  59.4 us (84%)
  starting transfers between devices  9.53 us (14%)
  between operations  0.87 us (1%)
    pallas_call x3, Pallas kernels, prefill_part(): pl.pallas_call(functools.partial(prefill_kernel, tokens, first=first, pac...  50.4 us
    pallas_call x1, Pallas kernels, small_part(): pl.pallas_call(small_kernel, grid_spec=pltpu.PrefetchScalarGridSpec(num_s...  7.18 us
    all_to_all x1, starting transfers between devices, per_device(): lax.all_to_all(sent, 'replica', split_axis=0, concat_axis=0, tiled=True)  6.45 us
    ppermute x2, starting transfers between devices, per_device(): lax.ppermute(part, 'tensor', [(i, (i + shift) % ranks) for i in range(ran...  3.08 us
    pallas_call x1, Pallas kernels, finish_part(): pl.pallas_call(functools.partial(finish_kernel, ranks), grid_spec=pltpu.P...  1.82 us
  transfers between devices with their start and end apart: 3, of which 0 were waited for; matrix products, arithmetic and copies ran while one was open for 0% of the time, Pallas kernels for 53%

profile of v1, /device:TPU:0, one launch (start us, length us, event | category | flops | bytes accessed | tf_op | source)
XLA Modules:
  0.0 69.8 jit_solution(17350604380173546090)
XLA Ops:
  0.6 7.2 %small.1 = (bf16[2,4096]{1,0:T(2,128)(2,1)}, bf16[16,32,128]{2,1,0:T(8,128)(2,1)}) custom-call(s32[6]{0:T(128)} %over_pages.1, s32[2,4]{1,0:T(2,128)} %dec_pages.1, s32[6]{0:T(128)} %over_len.1, s32[2]{0:T(128)} %dec_len.1, s32[6]{0:T(128)} %dest_ref.1, bf16[6,4096]{1,0:T(8,128)(2,1)} %over_ref.1, bf16[2,4096]{1,0:T(2,128)(2,1)} %decq_ref.1, ...), custom_call_target="tpu_custom_call" | custom-call | flops 234881024 | bytes 3670016 | tf_op jit(solution)/shard_map/small/pallas_call | solution.py:242
  7.8 13.2 %prefill.4 = bf16[192,2048]{1,0:T(8,128)(2,1)} custom-call(s32[1]{0:T(128)} %bitcast.2.blk_ref, s32[19]{0:T(128)} %bitcast.3, bf16[384,4096]{1,0:T(8,128)(2,1)} %q_ref.5, bf16[4224,512]{1,0:T(8,128)(2,1)} %k_hbm.7, bf16[4224,512]{1,0:T(8,128)(2,1)} %v_hbm.7), custom_call_target="tpu_custom_call" | custom-call | flops 3825205248 | bytes 4063232 | tf_op jit(solution)/shard_map/prefill/pallas_call | solution.py:145
  21.1 3.0 %collective-permute-start = (bf16[192,2048]{1,0:T(8,128)(2,1)}, bf16[192,2048]{1,0:T(8,128)(2,1)S(1)}, u32[]{:S(2)}, u32[]{:S(2)}) collective-permute-start(bf16[192,2048]{1,0:T(8,128)(2,1)} %prefill.4), channel_id=1, source_target_pairs={{0,1},{1,0},{2,3},{3,2},{4,5},{5,4},{6,7},{7,6},{8,9},{9,8},{10,11... | collective-permute-start | bytes 2359304 | tf_op jit(solution)/shard_map/ppermute | solution.py:369
  24.1 13.2 %prefill.5 = bf16[192,2048]{1,0:T(8,128)(2,1)} custom-call(s32[1]{0:T(128)} %bitcast.2.blk_ref, s32[19]{0:T(128)} %bitcast.4, bf16[384,4096]{1,0:T(8,128)(2,1)} %q_ref.5, bf16[4224,512]{1,0:T(8,128)(2,1)} %k_hbm.7, bf16[4224,512]{1,0:T(8,128)(2,1)} %v_hbm.7), custom_call_target="tpu_custom_call" | custom-call | flops 3825205248 | bytes 4063232 | tf_op jit(solution)/shard_map/prefill/pallas_call | solution.py:145
  37.3 0.1 collective-permute-start.1
  37.4 6.4 %all-to-all-start = ((bf16[16,32,128]{2,1,0:T(8,128)(2,1)}), bf16[16,32,128]{2,1,0:T(8,128)(2,1)S(1)}, u32[]{:S(2)}, u32[]{:S(2)}) async-start(bf16[16,32,128]{2,1,0:T(8,128)(2,1)} %get-tuple-element.10), calls=%async_computation | async-start | bytes 262144 | tf_op jit(solution)/shard_map/all_to_all | solution.py:359
  43.8 23.9 %prefill.3.big_ref = bf16[192,8192]{1,0:T(8,128)(2,1)} custom-call(s32[1]{0:T(128)} %bitcast.blk_ref.rank_ref, s32[19]{0:T(128)} %bitcast.5, bf16[384,4096]{1,0:T(8,128)(2,1)} %q_ref.5, bf16[4224,512]{1,0:T(8,128)(2,1)} %k_hbm.7, bf16[4224,512]{1,0:T(8,128)(2,1)} %v_hbm.7), custom_call_target="tpu_custom_call" | custom-call | flops 7650410496 | bytes 8126464 | tf_op jit(solution)/shard_map/prefill/pallas_call | solution.py:145
  67.8 0.0 all-to-all-done.rows_ref
  67.8 0.0 collective-permute-done.refs_0_
  67.8 0.0 collective-permute-done.1.refs_1_
  67.8 1.8 %finish.1 = (bf16[192,8192]{1,0:T(8,128)(2,1)}, bf16[16,4096]{1,0:T(8,128)(2,1)}) custom-call(s32[1]{0:T(128)} %bitcast.blk_ref.rank_ref, bf16[16,32,128]{2,1,0:T(8,128)(2,1)S(1)} %all-to-all-done.rows_ref, bf16[192,8192]{1,0:T(8,128)(2,1)} %prefill.3.big_ref, bf16[192,2048]{1,0:T(8,128)(2,1)S(1)} %collective-permute-done.refs_0_, ...), custom_call_target="tpu_custom_call", output_to_operand_aliasing={{0}: (2, {})} | custom-call | bytes 3407872 | tf_op jit(solution)/shard_map/finish/pallas_call | solution.py:302
Async XLA Ops:
  21.1 46.7 %collective-permute-start = (bf16[192,2048]{1,0:T(8,128)(2,1)}, bf16[192,2048]{1,0:T(8,128)(2,1)S(1)}, u32[]{:S(2)}, u32[]{:S(2)}) collective-permute-start(bf16[192,2048]{1,0:T(8,128)(2,1)} %prefill.4), channel_id=1, source_target_pairs={{0,1},{1,0},{2,3},{3,2},{4,5},{5,4},{6,7},{7,6},{8,9},{9,8},{10,11... | collective-permute-start | bytes 2359304 | tf_op jit(solution)/shard_map/ppermute | solution.py:369
  37.3 30.5 %collective-permute-start.1 = (bf16[192,2048]{1,0:T(8,128)(2,1)}, bf16[192,2048]{1,0:T(8,128)(2,1)S(1)}, u32[]{:S(2)}, u32[]{:S(2)}) collective-permute-start(bf16[192,2048]{1,0:T(8,128)(2,1)} %prefill.5), channel_id=1, source_target_pairs={{0,1},{1,0},{2,3},{3,2},{4,5},{5,4},{6,7},{7,6},{8,9},{9,8},{10,11... | collective-permute-start | bytes 2359304 | tf_op jit(solution)/shard_map/ppermute | solution.py:369
  37.4 30.4 %all-to-all-start = ((bf16[16,32,128]{2,1,0:T(8,128)(2,1)}), bf16[16,32,128]{2,1,0:T(8,128)(2,1)S(1)}, u32[]{:S(2)}, u32[]{:S(2)}) async-start(bf16[16,32,128]{2,1,0:T(8,128)(2,1)} %get-tuple-element.10), calls=%async_computation | async-start | bytes 262144 | tf_op jit(solution)/shard_map/all_to_all | solution.py:359

commit v2 on v0

--- a/solution.py
+++ b/solution.py
@@ -40,20 +40,22 @@
     def fetch(head):
         cols = pl.ds(pl.multiple_of((first + head) * D_HEAD, D_HEAD), D_HEAD)
 
-        def one(j, _):
-            src = pl.ds(pl.multiple_of(pages_ref[j] * PAGE, PAGE), PAGE)
-            dst = pl.ds(pl.multiple_of(j * PAGE, PAGE), PAGE)
-            pltpu.make_async_copy(k_hbm.at[src, cols], kbuf.at[head, dst], sem.at[head, 0]).start()
-            pltpu.make_async_copy(v_hbm.at[src, cols], vbuf.at[head, dst], sem.at[head, 1]).start()
-            return 0
-
-        lax.fori_loop(0, count, one, 0)
-
-    def keys_ready(head):
-        pltpu.make_async_copy(kbuf.at[head], kbuf.at[head], sem.at[head, 0]).wait()
-
-    def values_ready(head):
-        pltpu.make_async_copy(vbuf.at[head], vbuf.at[head], sem.at[head, 1]).wait()
+        for kind, (pool, buf) in enumerate(((k_hbm, kbuf), (v_hbm, vbuf))):
+            for i, (start, size) in enumerate(pieces):
+
+                def one(j, _):
+                    src = pl.ds(pl.multiple_of(pages_ref[j] * PAGE, PAGE), PAGE)
+                    dst = pl.ds(pl.multiple_of(j * PAGE, PAGE), PAGE)
+                    pltpu.make_async_copy(
+                        pool.at[src, cols], buf.at[head, dst], sem.at[head, kind, i]
+                    ).start()
+                    return 0
+
+                lax.fori_loop(start // PAGE, (start + size) // PAGE, one, 0)
+
+    def ready(head, kind, i):
+        part = (kbuf, vbuf)[kind].at[head, pl.ds(*pieces[i])]
+        pltpu.make_async_copy(part, part, sem.at[head, kind, i]).wait()
 
     def columns(unit, h):
         return pl.ds(pl.multiple_of((unit * pack + h) * D_HEAD, D_HEAD), D_HEAD)
@@ -77,11 +79,11 @@
         def _():
             fetch(head + 1)
 
-        @pl.when(u % units == 0)
-        def _():
-            keys_ready(head)
-
         for i, (start, size) in enumerate(pieces):
+
+            @pl.when(u % units == 0)
+            def _(i=i):
+                ready(head, 0, i)
 
             @tops(u)
             def _(i=i, start=start, size=size):
@@ -103,11 +105,11 @@
                     peak = jnp.broadcast_to(peak, top.shape)
                 top[...] = peak
 
-        @pl.when(u % units == 0)
-        def _():
-            values_ready(head)
-
         for i, (start, size) in enumerate(pieces):
+
+            @pl.when(u % units == 0)
+            def _(i=i):
+                ready(head, 1, i)
 
             @tops(u)
             def _(i=i, start=start, size=size):
@@ -156,7 +158,7 @@
                 pltpu.VMEM((pack * rows, span), jnp.float32),
                 pltpu.VMEM((pack * rows, D_HEAD), jnp.float32),
                 pltpu.VMEM((pack * rows, 2 * D_HEAD), jnp.float32),
-                pltpu.SemaphoreType.DMA((heads, 2)),
+                pltpu.SemaphoreType.DMA((heads, 2, len(chunks_of(span - tokens, tokens)))),
             ],
         ),
         out_shape=jax.ShapeDtypeStruct((rows, total * width), q.dtype),
@@ -180,12 +182,13 @@
     keys = count * PAGE
     heads = q_all.shape[1] // D_HEAD
 
-    for j in range(count):
-        page = over_pages[j] if j < over else dec_pages[(j - over) // per, (j - over) % per]
-        src = pl.ds(pl.multiple_of(page * PAGE, PAGE), PAGE)
-        dst = pl.ds(j * PAGE, PAGE)
-        pltpu.make_async_copy(k_hbm.at[src], kbuf.at[dst], sem.at[0]).start()
-        pltpu.make_async_copy(v_hbm.at[src], vbuf.at[dst], sem.at[1]).start()
+    for kind, (pool, buf) in enumerate(((k_hbm, kbuf), (v_hbm, vbuf))):
+        for j in range(count):
+            page = over_pages[j] if j < over else dec_pages[(j - over) // per, (j - over) % per]
+            src = pl.ds(pl.multiple_of(page * PAGE, PAGE), PAGE)
+            pltpu.make_async_copy(
+                pool.at[src], buf.at[pl.ds(j * PAGE, PAGE)], sem.at[kind]
+            ).start()
 
     if batch > over + dec:
         q_all[...] = jnp.zeros_like(q_all)
@@ -361,7 +364,7 @@
         step = min(heads, 2)
         for g in range(0, heads, step):
             part = prefill_part(
-                prefill_q, key_pool, value_pool, pages, blk, ranks, g, step, pack=4
+                prefill_q, key_pool, value_pool, pages, blk, ranks, g, step, pack=8
             )
             got.append(lax.ppermute(part, "tensor", [(i, (i + shift) % ranks) for i in range(ranks)]))
     own = rank[None].astype(jnp.int32)

time: 71.1 us -> 79.3 us (1.12)
  Pallas kernels: 60 us -> 68.2 us
    pallas_call x3, Pallas kernels: 51.5 us -> 60.3 us  [prefill_part(): pl.pallas_call(functools.partial(prefill_kernel, tokens, first=first, pac...]
  transfers between devices with their start and end apart: 3 -> 3, of which waited for: 0 -> 0; matrix products, arithmetic and copies ran while one was open for 0% -> 0% of each run, Pallas kernels for 54% -> 57%
where the time goes in v2:
time: 79.3 us; the launch traced here: 78.6 us
  Pallas kernels  68.2 us (86%)
  starting transfers between devices  9.54 us (12%)
  between operations  0.87 us (1%)
    pallas_call x3, Pallas kernels, prefill_part(): pl.pallas_call(functools.partial(prefill_kernel, tokens, first=first, pac...  60.3 us
    all_to_all x1, starting transfers between devices, per_device(): lax.all_to_all(sent, 'replica', split_axis=0, concat_axis=0, tiled=True)  6.46 us
    pallas_call x1, Pallas kernels, small_part(): pl.pallas_call(small_kernel, grid_spec=pltpu.PrefetchScalarGridSpec(num_s...  6.16 us
    ppermute x2, starting transfers between devices, per_device(): lax.ppermute(part, 'tensor', [(i, (i + shift) % ranks) for i in range(ran...  3.08 us
    pallas_call x1, Pallas kernels, finish_part(): pl.pallas_call(functools.partial(finish_kernel, ranks), grid_spec=pltpu.P...  1.82 us
  transfers between devices with their start and end apart: 3, of which 0 were waited for; matrix products, arithmetic and copies ran while one was open for 0% of the time, Pallas kernels for 57%

profile of v2, /device:TPU:0, one launch (start us, length us, event | category | flops | bytes accessed | tf_op | source)
XLA Modules:
  0.0 78.6 jit_solution(5880617030070835994)
XLA Ops:
  0.6 6.2 %small.1 = (bf16[2,4096]{1,0:T(2,128)(2,1)}, bf16[16,32,128]{2,1,0:T(8,128)(2,1)}) custom-call(s32[6]{0:T(128)} %over_pages.1, s32[2,4]{1,0:T(2,128)} %dec_pages.1, s32[6]{0:T(128)} %over_len.1, s32[2]{0:T(128)} %dec_len.1, s32[6]{0:T(128)} %dest_ref.1, bf16[6,4096]{1,0:T(8,128)(2,1)} %over_ref.1, bf16[2,4096]{1,0:T(2,128)(2,1)} %decq_ref.1, ...), custom_call_target="tpu_custom_call" | custom-call | flops 234881024 | bytes 3670016 | tf_op jit(solution)/shard_map/small/pallas_call | solution.py:243
  6.8 15.6 %prefill.4 = bf16[192,2048]{1,0:T(8,128)(2,1)} custom-call(s32[1]{0:T(128)} %bitcast.2.blk_ref, s32[19]{0:T(128)} %bitcast.3, bf16[384,4096]{1,0:T(8,128)(2,1)} %q_ref.5, bf16[4224,512]{1,0:T(8,128)(2,1)} %k_hbm.7, bf16[4224,512]{1,0:T(8,128)(2,1)} %v_hbm.7), custom_call_target="tpu_custom_call" | custom-call | flops 3825205248 | bytes 4063232 | tf_op jit(solution)/shard_map/prefill/pallas_call | solution.py:144
  22.4 3.0 %collective-permute-start = (bf16[192,2048]{1,0:T(8,128)(2,1)}, bf16[192,2048]{1,0:T(8,128)(2,1)S(1)}, u32[]{:S(2)}, u32[]{:S(2)}) collective-permute-start(bf16[192,2048]{1,0:T(8,128)(2,1)} %prefill.4), channel_id=1, source_target_pairs={{0,1},{1,0},{2,3},{3,2},{4,5},{5,4},{6,7},{7,6},{8,9},{9,8},{10,11... | collective-permute-start | bytes 2359304 | tf_op jit(solution)/shard_map/ppermute | solution.py:369
  25.5 15.6 %prefill.5 = bf16[192,2048]{1,0:T(8,128)(2,1)} custom-call(s32[1]{0:T(128)} %bitcast.2.blk_ref, s32[19]{0:T(128)} %bitcast.4, bf16[384,4096]{1,0:T(8,128)(2,1)} %q_ref.5, bf16[4224,512]{1,0:T(8,128)(2,1)} %k_hbm.7, bf16[4224,512]{1,0:T(8,128)(2,1)} %v_hbm.7), custom_call_target="tpu_custom_call" | custom-call | flops 3825205248 | bytes 4063232 | tf_op jit(solution)/shard_map/prefill/pallas_call | solution.py:144
  41.1 0.1 collective-permute-start.1
  41.2 6.5 %all-to-all-start = ((bf16[16,32,128]{2,1,0:T(8,128)(2,1)}), bf16[16,32,128]{2,1,0:T(8,128)(2,1)S(1)}, u32[]{:S(2)}, u32[]{:S(2)}) async-start(bf16[16,32,128]{2,1,0:T(8,128)(2,1)} %get-tuple-element.10), calls=%async_computation | async-start | bytes 262144 | tf_op jit(solution)/shard_map/all_to_all | solution.py:359
  47.7 29.0 %prefill.3.big_ref = bf16[192,8192]{1,0:T(8,128)(2,1)} custom-call(s32[1]{0:T(128)} %bitcast.blk_ref.rank_ref, s32[19]{0:T(128)} %bitcast.5, bf16[384,4096]{1,0:T(8,128)(2,1)} %q_ref.5, bf16[4224,512]{1,0:T(8,128)(2,1)} %k_hbm.7, bf16[4224,512]{1,0:T(8,128)(2,1)} %v_hbm.7), custom_call_target="tpu_custom_call" | custom-call | flops 7650410496 | bytes 8126464 | tf_op jit(solution)/shard_map/prefill/pallas_call | solution.py:144
  76.6 0.0 all-to-all-done.rows_ref
  76.6 0.0 collective-permute-done.refs_0_
  76.7 0.0 collective-permute-done.1.refs_1_
  76.7 1.8 %finish.1 = (bf16[192,8192]{1,0:T(8,128)(2,1)}, bf16[16,4096]{1,0:T(8,128)(2,1)}) custom-call(s32[1]{0:T(128)} %bitcast.blk_ref.rank_ref, bf16[16,32,128]{2,1,0:T(8,128)(2,1)S(1)} %all-to-all-done.rows_ref, bf16[192,8192]{1,0:T(8,128)(2,1)} %prefill.3.big_ref, bf16[192,2048]{1,0:T(8,128)(2,1)S(1)} %collective-permute-done.refs_0_, ...), custom_call_target="tpu_custom_call", output_to_operand_aliasing={{0}: (2, {})} | custom-call | bytes 3407872 | tf_op jit(solution)/shard_map/finish/pallas_call | solution.py:302
Async XLA Ops:
  22.4 54.2 %collective-permute-start = (bf16[192,2048]{1,0:T(8,128)(2,1)}, bf16[192,2048]{1,0:T(8,128)(2,1)S(1)}, u32[]{:S(2)}, u32[]{:S(2)}) collective-permute-start(bf16[192,2048]{1,0:T(8,128)(2,1)} %prefill.4), channel_id=1, source_target_pairs={{0,1},{1,0},{2,3},{3,2},{4,5},{5,4},{6,7},{7,6},{8,9},{9,8},{10,11... | collective-permute-start | bytes 2359304 | tf_op jit(solution)/shard_map/ppermute | solution.py:369
  41.1 35.5 %collective-permute-start.1 = (bf16[192,2048]{1,0:T(8,128)(2,1)}, bf16[192,2048]{1,0:T(8,128)(2,1)S(1)}, u32[]{:S(2)}, u32[]{:S(2)}) collective-permute-start(bf16[192,2048]{1,0:T(8,128)(2,1)} %prefill.5), channel_id=1, source_target_pairs={{0,1},{1,0},{2,3},{3,2},{4,5},{5,4},{6,7},{7,6},{8,9},{9,8},{10,11... | collective-permute-start | bytes 2359304 | tf_op jit(solution)/shard_map/ppermute | solution.py:369
  41.2 35.5 %all-to-all-start = ((bf16[16,32,128]{2,1,0:T(8,128)(2,1)}), bf16[16,32,128]{2,1,0:T(8,128)(2,1)S(1)}, u32[]{:S(2)}, u32[]{:S(2)}) async-start(bf16[16,32,128]{2,1,0:T(8,128)(2,1)} %get-tuple-element.10), calls=%async_computation | async-start | bytes 262144 | tf_op jit(solution)/shard_map/all_to_all | solution.py:359

commit v3 on v0

--- a/solution.py
+++ b/solution.py
@@ -40,14 +40,17 @@
     def fetch(head):
         cols = pl.ds(pl.multiple_of((first + head) * D_HEAD, D_HEAD), D_HEAD)
 
-        def one(j, _):
-            src = pl.ds(pl.multiple_of(pages_ref[j] * PAGE, PAGE), PAGE)
-            dst = pl.ds(pl.multiple_of(j * PAGE, PAGE), PAGE)
-            pltpu.make_async_copy(k_hbm.at[src, cols], kbuf.at[head, dst], sem.at[head, 0]).start()
-            pltpu.make_async_copy(v_hbm.at[src, cols], vbuf.at[head, dst], sem.at[head, 1]).start()
-            return 0
-
-        lax.fori_loop(0, count, one, 0)
+        for kind, (pool, buf) in enumerate(((k_hbm, kbuf), (v_hbm, vbuf))):
+
+            def one(j, _):
+                src = pl.ds(pl.multiple_of(pages_ref[j] * PAGE, PAGE), PAGE)
+                dst = pl.ds(pl.multiple_of(j * PAGE, PAGE), PAGE)
+                pltpu.make_async_copy(
+                    pool.at[src, cols], buf.at[head, dst], sem.at[head, kind]
+                ).start()
+                return 0
+
+            lax.fori_loop(0, count, one, 0)
 
     def keys_ready(head):
         pltpu.make_async_copy(kbuf.at[head], kbuf.at[head], sem.at[head, 0]).wait()
@@ -180,12 +183,13 @@
     keys = count * PAGE
     heads = q_all.shape[1] // D_HEAD
 
-    for j in range(count):
-        page = over_pages[j] if j < over else dec_pages[(j - over) // per, (j - over) % per]
-        src = pl.ds(pl.multiple_of(page * PAGE, PAGE), PAGE)
-        dst = pl.ds(j * PAGE, PAGE)
-        pltpu.make_async_copy(k_hbm.at[src], kbuf.at[dst], sem.at[0]).start()
-        pltpu.make_async_copy(v_hbm.at[src], vbuf.at[dst], sem.at[1]).start()
+    for kind, (pool, buf) in enumerate(((k_hbm, kbuf), (v_hbm, vbuf))):
+        for j in range(count):
+            page = over_pages[j] if j < over else dec_pages[(j - over) // per, (j - over) % per]
+            src = pl.ds(pl.multiple_of(page * PAGE, PAGE), PAGE)
+            pltpu.make_async_copy(
+                pool.at[src], buf.at[pl.ds(j * PAGE, PAGE)], sem.at[kind]
+            ).start()
 
     if batch > over + dec:
         q_all[...] = jnp.zeros_like(q_all)
@@ -361,7 +365,7 @@
         step = min(heads, 2)
         for g in range(0, heads, step):
             part = prefill_part(
-                prefill_q, key_pool, value_pool, pages, blk, ranks, g, step, pack=4
+                prefill_q, key_pool, value_pool, pages, blk, ranks, g, step, pack=8
             )
             got.append(lax.ppermute(part, "tensor", [(i, (i + shift) % ranks) for i in range(ranks)]))
     own = rank[None].astype(jnp.int32)

time: 71.1 us -> 69.5 us (0.977)
  Pallas kernels: 60 us -> 58.4 us
    pallas_call x3, Pallas kernels: 51.5 us -> 50.4 us  [prefill_part(): pl.pallas_call(functools.partial(prefill_kernel, tokens, first=first, pac...]
where the time goes in v3:
time: 69.5 us; the launch traced here: 68.8 us
  Pallas kernels  58.4 us (84%)
  starting transfers between devices  9.54 us (14%)
  between operations  0.87 us (1%)
    pallas_call x3, Pallas kernels, prefill_part(): pl.pallas_call(functools.partial(prefill_kernel, tokens, first=first, pac...  50.4 us
    all_to_all x1, starting transfers between devices, per_device(): lax.all_to_all(sent, 'replica', split_axis=0, concat_axis=0, tiled=True)  6.47 us
    pallas_call x1, Pallas kernels, small_part(): pl.pallas_call(small_kernel, grid_spec=pltpu.PrefetchScalarGridSpec(num_s...  6.16 us
    ppermute x2, starting transfers between devices, per_device(): lax.ppermute(part, 'tensor', [(i, (i + shift) % ranks) for i in range(ran...  3.08 us
    pallas_call x1, Pallas kernels, finish_part(): pl.pallas_call(functools.partial(finish_kernel, ranks), grid_spec=pltpu.P...  1.82 us
  transfers between devices with their start and end apart: 3, of which 0 were waited for; matrix products, arithmetic and copies ran while one was open for 0% of the time, Pallas kernels for 54%

profile of v3, /device:TPU:0, one launch (start us, length us, event | category | flops | bytes accessed | tf_op | source)
XLA Modules:
  0.0 68.8 jit_solution(4419567730403273145)
XLA Ops:
  0.6 6.2 %small.1 = (bf16[2,4096]{1,0:T(2,128)(2,1)}, bf16[16,32,128]{2,1,0:T(8,128)(2,1)}) custom-call(s32[6]{0:T(128)} %over_pages.1, s32[2,4]{1,0:T(2,128)} %dec_pages.1, s32[6]{0:T(128)} %over_len.1, s32[2]{0:T(128)} %dec_len.1, s32[6]{0:T(128)} %dest_ref.1, bf16[6,4096]{1,0:T(8,128)(2,1)} %over_ref.1, bf16[2,4096]{1,0:T(2,128)(2,1)} %decq_ref.1, ...), custom_call_target="tpu_custom_call" | custom-call | flops 234881024 | bytes 3670016 | tf_op jit(solution)/shard_map/small/pallas_call | solution.py:244
  6.8 13.2 %prefill.4 = bf16[192,2048]{1,0:T(8,128)(2,1)} custom-call(s32[1]{0:T(128)} %bitcast.2.blk_ref, s32[19]{0:T(128)} %bitcast.3, bf16[384,4096]{1,0:T(8,128)(2,1)} %q_ref.5, bf16[4224,512]{1,0:T(8,128)(2,1)} %k_hbm.7, bf16[4224,512]{1,0:T(8,128)(2,1)} %v_hbm.7), custom_call_target="tpu_custom_call" | custom-call | flops 3825205248 | bytes 4063232 | tf_op jit(solution)/shard_map/prefill/pallas_call | solution.py:145
  20.0 3.0 %collective-permute-start = (bf16[192,2048]{1,0:T(8,128)(2,1)}, bf16[192,2048]{1,0:T(8,128)(2,1)S(1)}, u32[]{:S(2)}, u32[]{:S(2)}) collective-permute-start(bf16[192,2048]{1,0:T(8,128)(2,1)} %prefill.4), channel_id=1, source_target_pairs={{0,1},{1,0},{2,3},{3,2},{4,5},{5,4},{6,7},{7,6},{8,9},{9,8},{10,11... | collective-permute-start | bytes 2359304 | tf_op jit(solution)/shard_map/ppermute | solution.py:370
  23.0 13.2 %prefill.5 = bf16[192,2048]{1,0:T(8,128)(2,1)} custom-call(s32[1]{0:T(128)} %bitcast.2.blk_ref, s32[19]{0:T(128)} %bitcast.4, bf16[384,4096]{1,0:T(8,128)(2,1)} %q_ref.5, bf16[4224,512]{1,0:T(8,128)(2,1)} %k_hbm.7, bf16[4224,512]{1,0:T(8,128)(2,1)} %v_hbm.7), custom_call_target="tpu_custom_call" | custom-call | flops 3825205248 | bytes 4063232 | tf_op jit(solution)/shard_map/prefill/pallas_call | solution.py:145
  36.3 0.1 collective-permute-start.1
  36.3 6.5 %all-to-all-start = ((bf16[16,32,128]{2,1,0:T(8,128)(2,1)}), bf16[16,32,128]{2,1,0:T(8,128)(2,1)S(1)}, u32[]{:S(2)}, u32[]{:S(2)}) async-start(bf16[16,32,128]{2,1,0:T(8,128)(2,1)} %get-tuple-element.10), calls=%async_computation | async-start | bytes 262144 | tf_op jit(solution)/shard_map/all_to_all | solution.py:360
  42.8 23.9 %prefill.3.big_ref = bf16[192,8192]{1,0:T(8,128)(2,1)} custom-call(s32[1]{0:T(128)} %bitcast.blk_ref.rank_ref, s32[19]{0:T(128)} %bitcast.5, bf16[384,4096]{1,0:T(8,128)(2,1)} %q_ref.5, bf16[4224,512]{1,0:T(8,128)(2,1)} %k_hbm.7, bf16[4224,512]{1,0:T(8,128)(2,1)} %v_hbm.7), custom_call_target="tpu_custom_call" | custom-call | flops 7650410496 | bytes 8126464 | tf_op jit(solution)/shard_map/prefill/pallas_call | solution.py:145
  66.8 0.0 all-to-all-done.rows_ref
  66.8 0.0 collective-permute-done.refs_0_
  66.8 0.0 collective-permute-done.1.refs_1_
  66.8 1.8 %finish.1 = (bf16[192,8192]{1,0:T(8,128)(2,1)}, bf16[16,4096]{1,0:T(8,128)(2,1)}) custom-call(s32[1]{0:T(128)} %bitcast.blk_ref.rank_ref, bf16[16,32,128]{2,1,0:T(8,128)(2,1)S(1)} %all-to-all-done.rows_ref, bf16[192,8192]{1,0:T(8,128)(2,1)} %prefill.3.big_ref, bf16[192,2048]{1,0:T(8,128)(2,1)S(1)} %collective-permute-done.refs_0_, ...), custom_call_target="tpu_custom_call", output_to_operand_aliasing={{0}: (2, {})} | custom-call | bytes 3407872 | tf_op jit(solution)/shard_map/finish/pallas_call | solution.py:303
Async XLA Ops:
  20.0 46.7 %collective-permute-start = (bf16[192,2048]{1,0:T(8,128)(2,1)}, bf16[192,2048]{1,0:T(8,128)(2,1)S(1)}, u32[]{:S(2)}, u32[]{:S(2)}) collective-permute-start(bf16[192,2048]{1,0:T(8,128)(2,1)} %prefill.4), channel_id=1, source_target_pairs={{0,1},{1,0},{2,3},{3,2},{4,5},{5,4},{6,7},{7,6},{8,9},{9,8},{10,11... | collective-permute-start | bytes 2359304 | tf_op jit(solution)/shard_map/ppermute | solution.py:370
  36.3 30.5 %collective-permute-start.1 = (bf16[192,2048]{1,0:T(8,128)(2,1)}, bf16[192,2048]{1,0:T(8,128)(2,1)S(1)}, u32[]{:S(2)}, u32[]{:S(2)}) collective-permute-start(bf16[192,2048]{1,0:T(8,128)(2,1)} %prefill.5), channel_id=1, source_target_pairs={{0,1},{1,0},{2,3},{3,2},{4,5},{5,4},{6,7},{7,6},{8,9},{9,8},{10,11... | collective-permute-start | bytes 2359304 | tf_op jit(solution)/shard_map/ppermute | solution.py:370
  36.3 30.4 %all-to-all-start = ((bf16[16,32,128]{2,1,0:T(8,128)(2,1)}), bf16[16,32,128]{2,1,0:T(8,128)(2,1)S(1)}, u32[]{:S(2)}, u32[]{:S(2)}) async-start(bf16[16,32,128]{2,1,0:T(8,128)(2,1)} %get-tuple-element.10), calls=%async_computation | async-start | bytes 262144 | tf_op jit(solution)/shard_map/all_to_all | solution.py:360
